TPU v7x, 32 devices: a whole 2x2x4 slice. The times are simulated.
32 devices in a mesh: seq: 16 (over z, y, core), head: 2 (over x).
Axes of the slice: x: 2, y: 2, z: 4, core: 2. Of those that a mesh axis runs over, the one named last changes fastest.
Arguments:
- queries: bfloat16 [11264, 8192], P('seq', 'head'), may hold values from -90 to 90
- encoded: bfloat16 [352, 32, 1024], P('seq', None, 'head'), may hold values from -6 to 6
- enc_gain: float32 [1024], P('head'), may hold values from 0.1 to 1.9
- w_kv: bfloat16 [1024, 2, 8192], P('seq', None, 'head'), may hold values from -0.1875 to 0.1875
- neighbour_block: int32 [352], replicated, may hold values from 0 to 175, as said below
- grad_context: bfloat16 [11264, 8192], P('seq', 'head'), may hold values from -6 to 6
Outputs:
- grad_queries: bfloat16 [11264, 8192], P('seq', 'head')
- grad_encoded: bfloat16 [352, 32, 1024], P('seq', None, 'head')
Inputs may be any that keep to these rules, and one draw needn't show every extreme that they name: `neighbour_block`: every query block has exactly 2 neighbours. The 22 neighbours of one shard of encoded go to 11 distinct owners of query blocks (block // 11), exactly 2 to each.
All inputs are finite; a program needn't handle non-finite values.
Results may differ from a plain program's by a relative error of at most 0.0065.
The roundings to bfloat16 on the way count: a program that leaves them out, or rounds other values in their place, can miss the bound.
Values may be sent and summed in bfloat16 or wider, within the bound.
A program may use at most 192 MiB of HBM per device.

v0:
```python
import functools

import jax
import jax.numpy as jnp
from jax import lax
from jax.experimental import pallas as pl
from jax.experimental.pallas import tpu as pltpu
from jax.sharding import PartitionSpec as P

HEAD_DIM = 128
SPAN = 64
NB = 2


def greet(n, heads, me, hd):
    barrier = pltpu.get_barrier_semaphore()
    for d in range(1, n):
        pl.semaphore_signal(
            barrier,
            inc=1,
            device_id={"seq": lax.rem(me + d, n)},
            device_id_type=pl.DeviceIdType.MESH,
        )
    for d in range(1, heads):
        pl.semaphore_signal(
            barrier,
            inc=1,
            device_id={"head": lax.rem(hd + d, heads)},
            device_id_type=pl.DeviceIdType.MESH,
        )
    pl.semaphore_wait(barrier, n + heads - 2)


def remote(src, dst, send, recv, **place):
    return pltpu.make_async_remote_copy(
        src_ref=src,
        dst_ref=dst,
        send_sem=send,
        recv_sem=recv,
        device_id=place,
        device_id_type=pl.DeviceIdType.MESH,
    )


def fold(values):
    total = values[:, :HEAD_DIM]
    for k in range(1, values.shape[1] // HEAD_DIM):
        total = total + values[:, k * HEAD_DIM : (k + 1) * HEAD_DIM]
    return total


def tail_kernel(
    n, heads, back_ref, take_ref, partial_ref, x_ref, rms_ref, gain_ref, out_ref,
    own, land, owned, packed, arrived, mine, others,
    own_sem, rs_send, rs_recv, a_send, a_recv, s_send, s_recv,
):
    me, hd = lax.axis_index("seq"), lax.axis_index("head")
    per_dev, nlen, ew_part = x_ref.shape
    cap = packed.shape[0] // n
    greet(n, heads, me, hd)

    def piece(which):
        return partial_ref.at[:, :, pl.ds(pl.multiple_of(which * ew_part, ew_part), ew_part)]

    sums = []
    for d in range(1, heads):
        to = lax.rem(hd + d, heads)
        sums.append(
            remote(piece(to), land.at[d - 1], rs_send.at[d - 1], rs_recv.at[d - 1], head=to)
        )
        sums[-1].start()
    local = pltpu.make_async_copy(piece(hd), own, own_sem)
    local.start()
    local.wait()
    for item in sums:
        item.wait_recv()

    @pl.loop(0, per_dev)
    def _(r):
        total = own[r]
        for d in range(1, heads):
            total = total + land[d - 1, r]
        owned[r] = total.astype(jnp.bfloat16)

    def parcel(d):
        to = lax.rem(me + d, n)
        return remote(
            packed.at[pl.ds(to * cap, cap)],
            arrived.at[pl.ds(me * cap, cap)],
            a_send.at[d - 1],
            a_recv.at[d - 1],
            seq=to,
        )

    for d in range(1, n):
        to = lax.rem(me + d, n)
        for t in range(cap):
            packed[to * cap + t] = owned[back_ref[to * cap + t]]
        parcel(d).start()
    for t in range(cap):
        arrived[me * cap + t] = owned[back_ref[me * cap + t]]
    for d in range(1, n):
        parcel(d).wait_recv()

    gain = gain_ref[...]

    @pl.loop(0, per_dev)
    def _(i):
        scaled = gain * arrived[take_ref[i]].astype(jnp.float32)
        mine[i] = fold(x_ref[i].astype(jnp.float32) * scaled)

    inners = []
    for d in range(1, heads):
        to = lax.rem(hd + d, heads)
        inners.append(remote(mine, others.at[d - 1], s_send.at[d - 1], s_recv.at[d - 1], head=to))
        inners[-1].start()
    for item in inners:
        item.wait_recv()

    @pl.loop(0, per_dev)
    def _(i):
        total = mine[i]
        for d in range(1, heads):
            total = total + others[d - 1, i]
        inner = jnp.sum(total, axis=-1, keepdims=True) / (ew_part * heads)
        scaled = gain * arrived[take_ref[i]].astype(jnp.float32)
        rms = rms_ref[i]
        x = x_ref[i].astype(jnp.float32)
        out_ref[i] = (rms * scaled - x * (rms * rms * rms * inner)).astype(jnp.bfloat16)

    for item in sums + inners:
        item.wait_send()
    for d in range(1, n):
        parcel(d).wait_send()


def tail(back, take, partial, x, rms, gain):
    n, heads = lax.axis_size("seq"), lax.axis_size("head")
    per_dev, nlen, ew_part = x.shape
    vmem = pl.BlockSpec(memory_space=pltpu.VMEM)
    smem = pl.BlockSpec(memory_space=pltpu.SMEM)
    slots = back.shape[0]
    return pl.pallas_call(
        functools.partial(tail_kernel, n, heads),
        out_shape=jax.ShapeDtypeStruct(x.shape, jnp.bfloat16),
        in_specs=[smem, smem, pl.BlockSpec(memory_space=pl.ANY), vmem, vmem, vmem],
        out_specs=vmem,
        scratch_shapes=[
            pltpu.VMEM(x.shape, jnp.float32),
            pltpu.VMEM((heads - 1,) + x.shape, jnp.float32),
            pltpu.VMEM(x.shape, jnp.bfloat16),
            pltpu.VMEM((slots, nlen, ew_part), jnp.bfloat16),
            pltpu.VMEM((slots, nlen, ew_part), jnp.bfloat16),
            pltpu.VMEM((per_dev, nlen, HEAD_DIM), jnp.float32),
            pltpu.VMEM((heads - 1, per_dev, nlen, HEAD_DIM), jnp.float32),
            pltpu.SemaphoreType.DMA,
            pltpu.SemaphoreType.DMA((heads - 1,)),
            pltpu.SemaphoreType.DMA((heads - 1,)),
            pltpu.SemaphoreType.DMA((n - 1,)),
            pltpu.SemaphoreType.DMA((n - 1,)),
            pltpu.SemaphoreType.DMA((heads - 1,)),
            pltpu.SemaphoreType.DMA((heads - 1,)),
        ],
        compiler_params=pltpu.CompilerParams(
            collective_id=1, has_side_effects=True, vmem_limit_bytes=32 * 1024 * 1024
        ),
    )(back, take, partial, x, rms, gain)


def routing(neighbour_block, device, n_seq, per_dev, blocks_dev, slot_cap):
    count_all = neighbour_block.shape[0]
    index = jnp.arange(count_all, dtype=jnp.int32)
    source = index // per_dev
    holder = neighbour_block // blocks_dev
    earlier = index[None, :] < index[:, None]
    same_pair = jnp.logical_and(
        source[:, None] == source[None, :], holder[:, None] == holder[None, :]
    )
    slot_rank = jnp.sum(jnp.logical_and(same_pair, earlier), axis=1)
    block_rank = jnp.sum(
        jnp.logical_and(neighbour_block[:, None] == neighbour_block[None, :], earlier), axis=1
    )
    row_here = (neighbour_block - device * blocks_dev) * NB + block_rank
    mine_here = holder == device
    rows_local = jnp.arange(per_dev, dtype=jnp.int32)
    slots_all = jnp.arange(n_seq * slot_cap, dtype=jnp.int32)
    select_all = jnp.logical_and(
        rows_local[:, None] == row_here[None, :], mine_here[None, :]
    ).astype(jnp.bfloat16)
    slot_table = ((source * slot_cap + slot_rank)[:, None] == slots_all[None, :]).astype(
        jnp.bfloat16
    )
    recv_select = jnp.dot(select_all, slot_table, preferred_element_type=jnp.float32).astype(
        jnp.bfloat16
    )
    send_target = lax.dynamic_slice_in_dim(holder * slot_cap + slot_rank, device * per_dev, per_dev)
    send_select = (slots_all[:, None] == send_target[None, :]).astype(jnp.bfloat16)
    back_row = jnp.sum(
        recv_select.astype(jnp.int32) * rows_local[:, None], axis=0, dtype=jnp.int32
    )
    return (send_select, recv_select, send_target.astype(jnp.int32), back_row)


ACROSS = 4
CORES = 2


def gather_kernel(n, w_ref, out_ref, own_sem, send_sem, recv_sem):
    me = lax.axis_index("seq")
    wide = n // (ACROSS * CORES)
    c = lax.rem(me, CORES)
    b = lax.rem(me // CORES, wide)
    a = me // (CORES * wide)

    def at(aa, bb, cc):
        return (aa * wide + bb) * CORES + cc

    barrier = pltpu.get_barrier_semaphore()
    partners = [at(lax.rem(a + 1, ACROSS), b, c), at(lax.rem(a + ACROSS - 1, ACROSS), b, c)]
    partners.append(at(a, lax.rem(b + 1, wide), c))
    if wide > 2:
        partners.append(at(a, lax.rem(b + wide - 1, wide), c))
    partners.append(at(a, b, 1 - c))
    for partner in partners:
        pl.semaphore_signal(
            barrier, inc=1, device_id={"seq": partner}, device_id_type=pl.DeviceIdType.MESH
        )
    pl.semaphore_wait(barrier, len(partners))

    def copy(slot, way, target, own):
        return pltpu.make_async_remote_copy(
            src_ref=w_ref if own else out_ref.at[slot],
            dst_ref=out_ref.at[slot],
            send_sem=send_sem.at[way, slot],
            recv_sem=recv_sem.at[slot],
            device_id={"seq": target},
            device_id_type=pl.DeviceIdType.MESH,
        )

    def moves(aa, bb, from_a, from_b, own, act):
        slot = at(aa, bb, c)
        if from_b == 0:
            if from_a >= 0:

                @pl.when(a + 1 < ACROSS)
                def _():
                    act(copy(slot, 0, at(a + 1, b, c), own))

            if from_a <= 0:

                @pl.when(a > 0)
                def _():
                    act(copy(slot, 1, at(a - 1, b, c), own))

        if from_b >= 0:

            @pl.when(b + 1 < wide)
            def _():
                act(copy(slot, 2, at(a, b + 1, c), own))

        if from_b <= 0:

            @pl.when(b > 0)
            def _():
                act(copy(slot, 3, at(a, b - 1, c), own))

        act(copy(slot, 4, at(a, b, 1 - c), own))

    def start(item):
        item.start()

    def wait_recv(slot):
        copy(slot, 4, at(a, b, 1 - c), False).wait_recv()

    def visit(each):
        for t in range(1, ACROSS + wide - 1):
            for j in range(0, min(t, wide - 1) + 1):
                k = t - j
                if k > ACROSS - 1:
                    continue
                for sa in (1, -1) if k else (0,):
                    for sb in (1, -1) if j else (0,):
                        aa, bb = a - sa * k, b - sb * j
                        here = None
                        if sa:
                            here = aa >= 0 if sa > 0 else aa < ACROSS
                        if sb:
                            more = bb >= 0 if sb > 0 else bb < wide
                            here = more if here is None else jnp.logical_and(here, more)

                        @pl.when(here)
                        def _(aa=aa, bb=bb, sa=sa, sb=sb):
                            each(aa, bb, sa, sb)

    own_copy = pltpu.make_async_copy(w_ref, out_ref.at[me], own_sem)
    moves(a, b, 0, 0, True, start)
    own_copy.start()

    def forward(aa, bb, sa, sb):
        wait_recv(at(aa, bb, c))
        moves(aa, bb, sa, sb, False, start)

    visit(forward)
    for aa in range(ACROSS):
        for bb in range(wide):
            wait_recv(at(aa, bb, 1 - c))
    own_copy.wait()
    moves(a, b, 0, 0, True, lambda item: item.wait_send())
    visit(lambda aa, bb, sa, sb: moves(aa, bb, sa, sb, False, lambda item: item.wait_send()))


def gather_weights(weights):
    n = lax.axis_size("seq")
    return pl.pallas_call(
        functools.partial(gather_kernel, n),
        out_shape=jax.ShapeDtypeStruct((n,) + weights.shape, weights.dtype),
        in_specs=[pl.BlockSpec(memory_space=pl.ANY)],
        out_specs=pl.BlockSpec(memory_space=pl.ANY),
        scratch_shapes=[
            pltpu.SemaphoreType.DMA,
            pltpu.SemaphoreType.DMA((5, n)),
            pltpu.SemaphoreType.DMA((n,)),
        ],
        compiler_params=pltpu.CompilerParams(collective_id=0, has_side_effects=True),
    )(weights)


GROUP = 4


def attention_kernel(q_ref, g_ref, kv_ref, gq_ref, gkv_ref):
    d_part = q_ref.shape[1]
    pair = 2 * HEAD_DIM
    scale = 1.0 / HEAD_DIM**0.5
    nt = (((1,), (1,)), ((), ()))
    tn = (((0,), (0,)), ((), ()))
    dot = functools.partial(lax.dot_general, preferred_element_type=jnp.float32)

    def diagonal(x):
        blank = jnp.zeros((x.shape[0], HEAD_DIM), x.dtype)
        upper = jnp.concatenate([x[:, :HEAD_DIM], blank], axis=1)
        lower = jnp.concatenate([blank, x[:, HEAD_DIM:]], axis=1)
        return jnp.concatenate([upper, lower], axis=0)

    @pl.loop(0, d_part // (GROUP * pair))
    def _(step):
        cols, cols_v = [], []
        for h in range(GROUP):
            start = pl.multiple_of((step * GROUP + h) * pair, pair)
            cols.append(pl.ds(start, pair))
            cols_v.append(pl.ds(pl.multiple_of(start + d_part, pair), pair))
        queries = [diagonal(q_ref[:, c]) for c in cols]
        grads = [diagonal(g_ref[:, c]) for c in cols]
        keys = [kv_ref[:, c] for c in cols]
        values = [kv_ref[:, c] for c in cols_v]
        scores = [dot(k, q, nt) * scale for k, q in zip(keys, queries)]
        dprobs = [dot(v, g, nt) for v, g in zip(values, grads)]
        low, dscores = [], []
        for s, dp in zip(scores, dprobs):
            weight = jnp.exp(s - jnp.max(s, axis=0, keepdims=True))
            probs = weight / jnp.sum(weight, axis=0, keepdims=True)
            delta = jnp.sum(probs * dp, axis=0, keepdims=True)
            low.append(probs.astype(jnp.bfloat16))
            dscores.append((probs * (dp - delta)).astype(jnp.bfloat16))
        grad_k = [dot(d, q, (((1,), (0,)), ((), ()))) * scale for d, q in zip(dscores, queries)]
        grad_v = [dot(p, g, (((1,), (0,)), ((), ()))) for p, g in zip(low, grads)]
        grad_q = [dot(d, k, tn) * scale for d, k in zip(dscores, keys)]
        for h in range(GROUP):
            gkv_ref[:, cols[h]] = grad_k[h].astype(jnp.bfloat16)
            gkv_ref[:, cols_v[h]] = grad_v[h].astype(jnp.bfloat16)
            both = jnp.concatenate(
                [grad_q[h][:SPAN, :HEAD_DIM], grad_q[h][SPAN:, HEAD_DIM:]], axis=1
            )
            gq_ref[:, cols[h]] = both.astype(jnp.bfloat16)


def attention(queries, grads, kv):
    rows, d_part = queries.shape
    keys_rows = kv.shape[0] * SPAN // rows

    def spec(height, width):
        return pl.BlockSpec((height, width), lambda i: (i, 0))

    return pl.pallas_call(
        attention_kernel,
        grid=(rows // SPAN,),
        out_shape=(
            jax.ShapeDtypeStruct(queries.shape, jnp.bfloat16),
            jax.ShapeDtypeStruct(kv.shape, jnp.bfloat16),
        ),
        in_specs=[spec(SPAN, d_part), spec(SPAN, d_part), spec(keys_rows, 2 * d_part)],
        out_specs=(spec(SPAN, d_part), spec(keys_rows, 2 * d_part)),
        compiler_params=pltpu.CompilerParams(vmem_limit_bytes=40 * 1024 * 1024),
    )(queries, grads, kv)


def shards(queries, encoded, enc_gain, w_kv, neighbour_block, grad_context):
    n_seq = lax.axis_size("seq")
    device = lax.axis_index("seq")
    per_dev, nlen, ew_part = encoded.shape
    ew_full = ew_part * lax.axis_size("head")
    tok_rows, d_part = queries.shape
    blocks_dev = tok_rows // SPAN
    slot_cap = (per_dev + n_seq - 1) // n_seq
    x_part = encoded.astype(jnp.float32)
    squares = lax.psum(jnp.sum(x_part * x_part, axis=-1), "head")
    inv_rms = lax.rsqrt(squares / ew_full + 1e-05)[..., None]
    normed = (x_part * inv_rms * enc_gain).astype(jnp.bfloat16)
    send_select, recv_select, send_target, back_row = routing(
        neighbour_block, device, n_seq, per_dev, blocks_dev, slot_cap
    )
    width_row = nlen * ew_part
    outgoing = jnp.dot(
        send_select, normed.reshape(per_dev, width_row), preferred_element_type=jnp.float32
    )
    outgoing = outgoing.astype(jnp.bfloat16).reshape(n_seq, slot_cap * width_row)
    incoming = lax.all_to_all(outgoing, "seq", split_axis=0, concat_axis=0, tiled=True)
    gathered = jnp.dot(
        recv_select,
        incoming.reshape(n_seq * slot_cap, width_row),
        preferred_element_type=jnp.float32,
    )
    owned = gathered.astype(jnp.bfloat16).reshape(per_dev, nlen, ew_part)
    full_rows = lax.all_gather(owned, "head", axis=2, tiled=True).reshape(per_dev * nlen, ew_full)
    flat = w_kv.reshape(w_kv.shape[0], 2 * d_part)
    weights = gather_weights(flat).reshape(ew_full, 2 * d_part)
    kv = jnp.dot(full_rows, weights, preferred_element_type=jnp.float32).astype(jnp.bfloat16)
    grad_queries, grad_kv = attention(queries, grad_context, kv)
    partial_rows = lax.dot_general(
        grad_kv, weights, (((1,), (1,)), ((), ())), preferred_element_type=jnp.float32
    )
    grad_encoded = tail(
        back_row,
        send_target,
        partial_rows.reshape(per_dev, nlen, ew_full),
        encoded,
        inv_rms,
        enc_gain[None, :],
    )
    return (grad_queries, grad_encoded)


def solution(mesh):
    return jax.shard_map(
        shards,
        mesh=mesh,
        in_specs=(
            P("seq", "head"),
            P("seq", None, "head"),
            P("head"),
            P("seq", None, "head"),
            P(),
            P("seq", "head"),
        ),
        out_specs=(P("seq", "head"), P("seq", None, "head")),
        check_vma=False,
    )
```

profile of v0, /device:TPU:13, one launch (start us, length us, event | category | flops | bytes accessed | tf_op | source)
XLA Modules:
  0.0 334.4 jit_solution(4754870945639873816)
XLA Ops:
  7.2 1.0 convert_reduce_fusion.1
  8.2 0.7 broadcast_compare_fusion
  8.9 1.3 fusion
  10.2 6.1 %psum.7 = f32[22,32]{1,0:T(8,128)S(1)} all-reduce(f32[22,32]{1,0:T(8,128)S(1)} %fusion), channel_id=1, replica_groups=mesh['seq'=16,'head'=2] {'head'}, use_global_device_ids=true, to_apply=%region_3.4 | all-reduce | flops 704 | bytes 5632 | tf_op jit(solution)/shard_map/psum | solution.py:406
  16.3 1.3 fusion.2
  17.6 0.1 pad
  17.7 0.4 copy.15
  18.2 0.3 convert_reduce_fusion
  18.4 0.7 multiply_add_fusion
  19.1 0.1 dynamic_slice.3.take_ref
  19.2 0.4 convolution_convert_fusion
  19.6 2.8 all_to_all.8
  22.4 0.5 broadcast.79
  22.9 8.4 %reduce.1 = bf16[16,32768]{1,0:T(8,128)(2,1)S(1)} reduce(bf16[16,1,32768]{2,1,0:T(2,128)(2,1)} %all_to_all.8, bf16[]{:T(256)} %broadcast.79), dimensions={1}, to_apply=%all_to_all.8.reduce_sub_computation | reduce | bytes 2097154 | tf_op jit(solution)/shard_map/all_to_all | solution.py:417
  31.3 1.6 reshape.78
  32.9 8.6 %all-to-all-start = ((bf16[16,2,16384]{2,1,0:T(2,128)(2,1)}), bf16[16,2,16384]{2,1,0:T(2,128)(2,1)S(1)}, u32[]{:S(2)}, u32[]{:S(2)}) async-start(bf16[16,2,16384]{2,1,0:T(2,128)(2,1)} %reshape.78), calls=%async_computation | async-start | bytes 2097152 | tf_op jit(solution)/shard_map/all_to_all | solution.py:417
  41.5 0.2 all-gather.2.cloned.1.call-start
  41.7 0.2 multiply_reduce_fusion
  42.0 24.4 %all-to-all-done = bf16[16,2,16384]{2,1,0:T(2,128)(2,1)S(1)} async-done(((bf16[16,2,16384]{2,1,0:T(2,128)(2,1)}), bf16[16,2,16384]{2,1,0:T(2,128)(2,1)S(1)}, u32[]{:S(2)}, u32[]{:S(2)}) %all-to-all-start) | async-done | bytes 1048608 | tf_op jit(solution)/shard_map/all_to_all | solution.py:417
  66.4 3.4 %reshape.79 = bf16[16,1,32768]{2,1,0:T(2,128)(2,1)} reshape(bf16[16,2,16384]{2,1,0:T(2,128)(2,1)S(1)} %all-to-all-done) | data formatting | bytes 2097152
  69.8 7.7 %reduce = bf16[16,32768]{1,0:T(8,128)(2,1)S(1)} reduce(bf16[16,1,32768]{2,1,0:T(2,128)(2,1)} %reshape.79, bf16[]{:T(256)} %constant.36), dimensions={1}, to_apply=%all_to_all.7.reduce_sub_computation | reduce | bytes 2097154 | tf_op jit(solution)/shard_map/all_to_all | solution.py:417
  77.5 0.5 reshape.71
  78.0 0.4 convolution_convert_fusion.1
  78.4 0.2 copy.16
  78.6 0.9 slice
  79.6 0.0 all-gather.2.cloned.1.call-update
  79.6 2.8 copy.17
  82.4 0.0 slice-start
  82.4 98.4 %shard_map.77 = bf16[16,64,8192]{2,1,0:T(8,128)(2,1)} custom-call(bf16[64,8192]{1,0:T(8,128)(2,1)} %bitcast.28), custom_call_target="tpu_custom_call" | custom-call | tf_op jit(solution)/shard_map/pallas_call | solution.py:314
  180.8 0.2 copy.14.rms_ref
  181.0 0.0 all-gather.2.cloned.1.call-done
  181.1 0.0 slice-start.1
  181.1 21.2 %convolution_convert_fusion.2.kv_ref = bf16[704,8192]{1,0:T(8,128)(2,1)} fusion(bf16[704,1024]{1,0:T(8,128)(2,1)} %bitcast.35, bf16[1024,8192]{1,0:T(8,128)(2,1)} %bitcast.26), kind=kOutput, calls=%fused_computation.2 | convolution fusion | flops 11816927232 | bytes 29753344 | tf_op jit(solution)/shard_map/dot_general | solution.py:427
  202.3 0.0 slice-done
  202.3 0.0 slice-done.1
  202.3 0.0 copy-start.1
  202.3 2.6 copy-done.1
  204.9 28.5 %shard_map.78 = (bf16[704,4096]{1,0:T(8,128)(2,1)}, bf16[704,8192]{1,0:T(8,128)(2,1)}) custom-call(bf16[704,4096]{1,0:T(8,128)(2,1)S(1)} %bitcast.24, bf16[704,4096]{1,0:T(8,128)(2,1)S(1)} %copy-done.1, bf16[704,8192]{1,0:T(8,128)(2,1)} %convolution_convert_fusion.2.kv_ref), custom_call_target="tpu_custom_call" | custom-call | tf_op jit(solution)/shard_map/pallas_call | solution.py:384
  233.4 0.0 copy-start
  233.4 0.0 copy-start.2
  233.4 17.5 %fusion.16.partial_ref = f32[22,32,1024]{2,1,0:T(8,128)S(1)} fusion(bf16[22,32,8192]{2,1,0:T(8,128)(2,1)} %bitcast.34, bf16[1024,8192,1]{1,0,2:T(8,128)(2,1)} %bitcast.27), kind=kOutput, calls=%fused_computation.40 | convolution fusion | flops 11811160064 | bytes 31195136 | tf_op jit(solution)/shard_map/dot_general | solution.py:429
  250.9 0.0 copy-done
  250.9 0.0 copy-done.2
  250.9 75.8 %shard_map.79 = bf16[22,32,512]{2,1,0:T(8,128)(2,1)S(1)} custom-call(s32[32]{0:T(128)S(1)} %get-tuple-element.12.back_ref, s32[22]{0:T(128)S(1)} %dynamic_slice.3.take_ref, f32[22,32,1024]{2,1,0:T(8,128)S(1)} %fusion.16.partial_ref, bf16[22,32,512]{2,1,0:T(8,128)(2,1)S(1)} %copy-done, f32[22,32,1]{2,1,0:T(8,128)S(1)} %copy.14.rms_ref, f32[1,512]{1,0:T(1,128)S(1)} %bitcast.25), custom_call_target="tpu_custom_call" | custom-call | tf_op jit(solution)/shard_map/pallas_call | solution.py:143
  326.7 0.9 copy.19
  (3 shorter events, 0.0 us)
Async XLA Ops:
  32.9 33.4 %all-to-all-start = ((bf16[16,2,16384]{2,1,0:T(2,128)(2,1)}), bf16[16,2,16384]{2,1,0:T(2,128)(2,1)S(1)}, u32[]{:S(2)}, u32[]{:S(2)}) async-start(bf16[16,2,16384]{2,1,0:T(2,128)(2,1)} %reshape.78), calls=%async_computation | async-start | bytes 2097152 | tf_op jit(solution)/shard_map/all_to_all | solution.py:417
  41.5 139.6 %all-gather.2.cloned.1.call-start = ((), (), s32[]{:S(2)}) async-start(), calls=%async_computation.1 | async-start | bytes 2162688 | tf_op jit(solution)/shard_map/all_gather | solution.py:424
  82.4 119.9 %slice-start = ((s8[5767168]{0:T(1024)(128)(4,1)}), s8[1572864]{0:T(1024)(128)(4,1)S(1)}, s32[]{:S(2)}) async-start(s8[5767168]{0:T(1024)(128)(4,1)} %bitcast.23), calls=%async_computation.2 | async-start | bytes 3145728
  181.1 21.2 %slice-start.1 = ((s8[5767168]{0:T(1024)(128)(4,1)}), s8[4194304]{0:T(1024)(128)(4,1)S(1)}, s32[]{:S(2)}) async-start(s8[5767168]{0:T(1024)(128)(4,1)} %bitcast.23), calls=%async_computation.3 | async-start | bytes 8388608
  202.3 2.6 copy-start.1
  233.4 17.5 %copy-start = (bf16[22,32,512]{2,1,0:T(8,128)(2,1)S(1)}, bf16[22,32,512]{2,1,0:T(8,128)(2,1)}, u32[]{:S(2)}) copy-start(bf16[22,32,512]{2,1,0:T(8,128)(2,1)} %x_ref.1) | copy-start | bytes 2162692
  233.4 17.5 %copy-start.2 = (f32[512]{0:T(512)S(1)}, f32[512]{0:T(512)}, u32[]{:S(2)}) copy-start(f32[512]{0:T(512)} %param.8) | copy-start | bytes 6148
Sparse Core Ops, SparseCore 0:
  79.7 24.2 all-gather.1
where the time goes:
time: 335 us; the launch traced here: 334 us
  Pallas kernels  203 us (61%)
  matrix products  39.7 us (12%)
  waiting for transfers between devices  24.4 us (7%)
  other arithmetic  21.4 us (6%)
  local copies, waits for them, and re-layouts  17.1 us (5%)
  between operations  14.2 us (4%)
  starting transfers between devices  8.79 us (3%)
  blocking collectives  6.07 us (2%)
    pallas_call x1, Pallas kernels, gather_weights(): pl.pallas_call(functools.partial(gather_kernel, n), out_shape=jax.ShapeDt...  98.4 us
    pallas_call x1, Pallas kernels, tail(): pl.pallas_call(functools.partial(tail_kernel, n, heads), out_shape=jax.Sh...  75.8 us
    pallas_call x1, Pallas kernels, attention(): pl.pallas_call(attention_kernel, grid=(rows // SPAN,), out_shape=(jax.Sha...  28.5 us
    all_to_all x1, waiting for transfers between devices, shards(): lax.all_to_all(outgoing, 'seq', split_axis=0, concat_axis=0, tiled=True)  24.4 us
    dot_general x1, matrix products, shards(): jnp.dot(full_rows, weights, preferred_element_type=jnp.float32)  21.2 us
    dot_general x1, matrix products, shards(): lax.dot_general(grad_kv, weights, (((1,), (1,)), ((), ())), preferred_ele...  17.5 us
    all_to_all x2, other arithmetic, shards(): lax.all_to_all(outgoing, 'seq', split_axis=0, concat_axis=0, tiled=True)  16.1 us
    unnamed x17, local copies, waits for them, and re-layouts  12.1 us
  transfers between devices with their start and end apart: 2, of which 1 were waited for; matrix products, arithmetic and copies ran while one was open for 1% of the time, Pallas kernels for 29%

commit v1 on v0

--- a/solution.py
+++ b/solution.py
@@ -194,19 +194,29 @@
         jnp.bfloat16
     )
     send_target = lax.dynamic_slice_in_dim(holder * slot_cap + slot_rank, device * per_dev, per_dev)
-    send_select = (slots_all[:, None] == send_target[None, :]).astype(jnp.bfloat16)
+    sent = slots_all[:, None] == send_target[None, :]
+    send_row = jnp.sum(jnp.where(sent, rows_local[None, :], 0), axis=1, dtype=jnp.int32)
+    take_row = jnp.sum(
+        recv_select.astype(jnp.int32) * slots_all[None, :], axis=1, dtype=jnp.int32
+    )
     back_row = jnp.sum(
         recv_select.astype(jnp.int32) * rows_local[:, None], axis=0, dtype=jnp.int32
     )
-    return (send_select, recv_select, send_target.astype(jnp.int32), back_row)
+    return (send_row, take_row, send_target.astype(jnp.int32), back_row)
 
 
 ACROSS = 4
 CORES = 2
 
 
-def gather_kernel(n, w_ref, out_ref, own_sem, send_sem, recv_sem):
-    me = lax.axis_index("seq")
+def gather_kernel(
+    n, heads, send_ref, take_ref, w_ref, x_ref, gain_ref, out_ref, full_ref, rms_ref,
+    mine, others, normed, packed, incoming, owned,
+    own_sem, send_sem, recv_sem, s_send, s_recv, a_send, a_recv, h_own, h_send, h_recv,
+):
+    me, hd = lax.axis_index("seq"), lax.axis_index("head")
+    per_dev, nlen, ew_part = x_ref.shape
+    cap = packed.shape[0] // n
     wide = n // (ACROSS * CORES)
     c = lax.rem(me, CORES)
     b = lax.rem(me // CORES, wide)
@@ -215,17 +225,7 @@
     def at(aa, bb, cc):
         return (aa * wide + bb) * CORES + cc
 
-    barrier = pltpu.get_barrier_semaphore()
-    partners = [at(lax.rem(a + 1, ACROSS), b, c), at(lax.rem(a + ACROSS - 1, ACROSS), b, c)]
-    partners.append(at(a, lax.rem(b + 1, wide), c))
-    if wide > 2:
-        partners.append(at(a, lax.rem(b + wide - 1, wide), c))
-    partners.append(at(a, b, 1 - c))
-    for partner in partners:
-        pl.semaphore_signal(
-            barrier, inc=1, device_id={"seq": partner}, device_id_type=pl.DeviceIdType.MESH
-        )
-    pl.semaphore_wait(barrier, len(partners))
+    greet(n, heads, me, hd)
 
     def copy(slot, way, target, own):
         return pltpu.make_async_remote_copy(
@@ -296,33 +296,121 @@
     moves(a, b, 0, 0, True, start)
     own_copy.start()
 
+    @pl.loop(0, per_dev)
+    def _(i):
+        x = x_ref[i].astype(jnp.float32)
+        mine[i] = fold(x * x)
+
+    squares = []
+    for d in range(1, heads):
+        to = lax.rem(hd + d, heads)
+        squares.append(remote(mine, others.at[d - 1], s_send.at[d - 1], s_recv.at[d - 1], head=to))
+        squares[-1].start()
+    for item in squares:
+        item.wait_recv()
+    gain = gain_ref[...]
+
+    @pl.loop(0, per_dev)
+    def _(i):
+        total = mine[i]
+        for d in range(1, heads):
+            total = total + others[d - 1, i]
+        mean = jnp.sum(total, axis=-1, keepdims=True) / (ew_part * heads)
+        rms = lax.rsqrt(mean + 1e-05)
+        rms_ref[i] = rms
+        normed[i] = (x_ref[i].astype(jnp.float32) * rms * gain).astype(jnp.bfloat16)
+
+    def parcel(d):
+        to = lax.rem(me + d, n)
+        return remote(
+            packed.at[pl.ds(to * cap, cap)],
+            incoming.at[pl.ds(me * cap, cap)],
+            a_send.at[d - 1],
+            a_recv.at[d - 1],
+            seq=to,
+        )
+
+    for d in range(1, n):
+        to = lax.rem(me + d, n)
+        for t in range(cap):
+            packed[to * cap + t] = normed[send_ref[to * cap + t]]
+        parcel(d).start()
+    for t in range(cap):
+        incoming[me * cap + t] = normed[send_ref[me * cap + t]]
+
     def forward(aa, bb, sa, sb):
         wait_recv(at(aa, bb, c))
         moves(aa, bb, sa, sb, False, start)
 
     visit(forward)
+    for d in range(1, n):
+        parcel(d).wait_recv()
+
+    @pl.loop(0, per_dev)
+    def _(r):
+        owned[r] = incoming[take_ref[r]]
+
+    columns = full_ref.at[:, :, pl.ds(pl.multiple_of(hd * ew_part, ew_part), ew_part)]
+    shares = []
+    for d in range(1, heads):
+        to = lax.rem(hd + d, heads)
+        shares.append(remote(owned, columns, h_send.at[d - 1], h_recv.at[d - 1], head=to))
+        shares[-1].start()
+    own_share = pltpu.make_async_copy(owned, columns, h_own)
+    own_share.start()
     for aa in range(ACROSS):
         for bb in range(wide):
             wait_recv(at(aa, bb, 1 - c))
     own_copy.wait()
+    own_share.wait()
+    for item in shares:
+        item.wait_recv()
+    for item in squares + shares:
+        item.wait_send()
+    for d in range(1, n):
+        parcel(d).wait_send()
     moves(a, b, 0, 0, True, lambda item: item.wait_send())
     visit(lambda aa, bb, sa, sb: moves(aa, bb, sa, sb, False, lambda item: item.wait_send()))
 
 
-def gather_weights(weights):
-    n = lax.axis_size("seq")
+def gather(send_row, take_row, weights, x, gain):
+    n, heads = lax.axis_size("seq"), lax.axis_size("head")
+    per_dev, nlen, ew_part = x.shape
+    slots = send_row.shape[0]
+    vmem = pl.BlockSpec(memory_space=pltpu.VMEM)
+    smem = pl.BlockSpec(memory_space=pltpu.SMEM)
+    anywhere = pl.BlockSpec(memory_space=pl.ANY)
     return pl.pallas_call(
-        functools.partial(gather_kernel, n),
-        out_shape=jax.ShapeDtypeStruct((n,) + weights.shape, weights.dtype),
-        in_specs=[pl.BlockSpec(memory_space=pl.ANY)],
-        out_specs=pl.BlockSpec(memory_space=pl.ANY),
+        functools.partial(gather_kernel, n, heads),
+        out_shape=(
+            jax.ShapeDtypeStruct((n,) + weights.shape, weights.dtype),
+            jax.ShapeDtypeStruct((per_dev, nlen, ew_part * heads), jnp.bfloat16),
+            jax.ShapeDtypeStruct((per_dev, nlen, 1), jnp.float32),
+        ),
+        in_specs=[smem, smem, anywhere, vmem, vmem],
+        out_specs=(anywhere, anywhere, vmem),
         scratch_shapes=[
+            pltpu.VMEM((per_dev, nlen, HEAD_DIM), jnp.float32),
+            pltpu.VMEM((heads - 1, per_dev, nlen, HEAD_DIM), jnp.float32),
+            pltpu.VMEM(x.shape, jnp.bfloat16),
+            pltpu.VMEM((slots, nlen, ew_part), jnp.bfloat16),
+            pltpu.VMEM((slots, nlen, ew_part), jnp.bfloat16),
+            pltpu.VMEM(x.shape, jnp.bfloat16),
             pltpu.SemaphoreType.DMA,
             pltpu.SemaphoreType.DMA((5, n)),
             pltpu.SemaphoreType.DMA((n,)),
+            pltpu.SemaphoreType.DMA((heads - 1,)),
+            pltpu.SemaphoreType.DMA((heads - 1,)),
+            pltpu.SemaphoreType.DMA((n - 1,)),
+            pltpu.SemaphoreType.DMA((n - 1,)),
+            pltpu.SemaphoreType.DMA,
+            pltpu.SemaphoreType.DMA((heads - 1,)),
+            pltpu.SemaphoreType.DMA((heads - 1,)),
         ],
-        compiler_params=pltpu.CompilerParams(collective_id=0, has_side_effects=True),
-    )(weights)
+        compiler_params=pltpu.CompilerParams(
+            collective_id=0, has_side_effects=True, vmem_limit_bytes=32 * 1024 * 1024
+        ),
+    )(send_row, take_row, weights, x, gain)
 
 
 GROUP = 4
@@ -402,28 +490,13 @@
     tok_rows, d_part = queries.shape
     blocks_dev = tok_rows // SPAN
     slot_cap = (per_dev + n_seq - 1) // n_seq
-    x_part = encoded.astype(jnp.float32)
-    squares = lax.psum(jnp.sum(x_part * x_part, axis=-1), "head")
-    inv_rms = lax.rsqrt(squares / ew_full + 1e-05)[..., None]
-    normed = (x_part * inv_rms * enc_gain).astype(jnp.bfloat16)
-    send_select, recv_select, send_target, back_row = routing(
+    send_row, take_row, send_target, back_row = routing(
         neighbour_block, device, n_seq, per_dev, blocks_dev, slot_cap
     )
-    width_row = nlen * ew_part
-    outgoing = jnp.dot(
-        send_select, normed.reshape(per_dev, width_row), preferred_element_type=jnp.float32
-    )
-    outgoing = outgoing.astype(jnp.bfloat16).reshape(n_seq, slot_cap * width_row)
-    incoming = lax.all_to_all(outgoing, "seq", split_axis=0, concat_axis=0, tiled=True)
-    gathered = jnp.dot(
-        recv_select,
-        incoming.reshape(n_seq * slot_cap, width_row),
-        preferred_element_type=jnp.float32,
-    )
-    owned = gathered.astype(jnp.bfloat16).reshape(per_dev, nlen, ew_part)
-    full_rows = lax.all_gather(owned, "head", axis=2, tiled=True).reshape(per_dev * nlen, ew_full)
     flat = w_kv.reshape(w_kv.shape[0], 2 * d_part)
-    weights = gather_weights(flat).reshape(ew_full, 2 * d_part)
+    weights, owned, inv_rms = gather(send_row, take_row, flat, encoded, enc_gain[None, :])
+    weights = weights.reshape(ew_full, 2 * d_part)
+    full_rows = owned.reshape(per_dev * nlen, ew_full)
     kv = jnp.dot(full_rows, weights, preferred_element_type=jnp.float32).astype(jnp.bfloat16)
     grad_queries, grad_kv = attention(queries, grad_context, kv)
     partial_rows = lax.dot_general(

time: 335 us -> 295 us (0.88)
  Pallas kernels: 203 us -> 241 us
  waiting for transfers between devices: 24.4 us -> 0 us
  other arithmetic: 21.4 us -> 2.73 us
  between operations: 14.2 us -> 0.71 us
  starting transfers between devices: 8.79 us -> 0 us
  blocking collectives: 6.07 us -> 0 us
  local copies, waits for them, and re-layouts: 17.1 us -> 12.9 us
    pallas_call x1, Pallas kernels: 98.4 us -> 125 us  [gather(): pl.pallas_call(functools.partial(gather_kernel, n, heads), out_shape=(jax...]
    all_to_all x1 -> x0, waiting for transfers between devices: 24.4 us -> none  [shards(): lax.all_to_all(outgoing, 'seq', split_axis=0, concat_axis=0, tiled=True)]
    all_to_all x2 -> x0, other arithmetic: 16.1 us -> none  [shards(): lax.all_to_all(outgoing, 'seq', split_axis=0, concat_axis=0, tiled=True)]
    pallas_call x1, Pallas kernels: 75.8 us -> 87.4 us  [tail(): pl.pallas_call(functools.partial(tail_kernel, n, heads), out_shape=jax.Sh...]
    all_to_all x1 -> x0, starting transfers between devices: 8.57 us -> none  [shards(): lax.all_to_all(outgoing, 'seq', split_axis=0, concat_axis=0, tiled=True)]
    psum x1 -> x0, blocking collectives: 6.07 us -> none  [shards(): squares = lax.psum(jnp.sum(x_part * x_part, axis=-1), 'head')]
    unnamed x17 -> x18, local copies, waits for them, and re-layouts: 12.1 us -> 12.8 us
  transfers between devices with their start and end apart: 2 -> 0, of which waited for: 1 -> 0; matrix products, arithmetic and copies ran while one was open for 1% -> 0% of each run, Pallas kernels for 29% -> 0%
where the time goes in v1:
time: 295 us
  Pallas kernels  241 us (82%)
  matrix products  38 us (13%)
  local copies, waits for them, and re-layouts  12.9 us (4%)
    pallas_call x1, Pallas kernels, gather(): pl.pallas_call(functools.partial(gather_kernel, n, heads), out_shape=(jax...  125 us
    pallas_call x1, Pallas kernels, tail(): pl.pallas_call(functools.partial(tail_kernel, n, heads), out_shape=jax.Sh...  87.4 us
    pallas_call x1, Pallas kernels, attention(): pl.pallas_call(attention_kernel, grid=(rows // SPAN,), out_shape=(jax.Sha...  28.6 us
    dot_general x1, matrix products, shards(): jnp.dot(full_rows, weights, preferred_element_type=jnp.float32)  20.2 us
    dot_general x1, matrix products, shards(): lax.dot_general(grad_kv, weights, (((1,), (1,)), ((), ())), preferred_ele...  17.4 us
    unnamed x18, local copies, waits for them, and re-layouts  12.8 us

profile of v1, /device:TPU:13, one launch (start us, length us, event | category | flops | bytes accessed | tf_op | source)
XLA Modules:
  0.0 295.1 jit_solution(10073640040374605642)
XLA Ops:
  0.6 1.0 convert_reduce_fusion
  1.6 0.7 broadcast_compare_fusion
  2.3 0.3 convert_reduce_fusion.1
  2.6 0.7 multiply_add_fusion
  3.3 0.3 multiply_reduce_fusion
  3.6 0.1 dynamic_slice.3.take_ref
  3.7 0.1 select_reduce_fusion.send_ref
  3.8 1.8 copy.8
  5.6 0.0 copy-start.1
  5.6 1.1 copy-done.1
  6.7 0.0 copy-start.3
  6.7 0.7 copy-done.3
  7.4 0.0 slice-start
  7.4 124.8 %shard_map.77 = (bf16[16,64,8192]{2,1,0:T(8,128)(2,1)S(1)}, bf16[22,32,1024]{2,1,0:T(8,128)(2,1)S(1)}, f32[22,32,1]{2,1,0:T(8,128)S(1)}) custom-call(s32[32]{0:T(128)S(1)} %select_reduce_fusion.send_ref, s32[22]{0:T(128)S(1)} %get-tuple-element.13.take_ref, bf16[64,8192]{1,0:T(8,128)(2,1)S(1)} %bitcast.14, bf16[22,32,512]{2,1,0:T(8,128)(2,1)S(1)} %copy-done.1, ...), custom_call_target="tpu_custom_call" | custom-call | tf_op jit(solution)/shard_map/pallas_call | solution.py:383
  132.2 0.0 copy-start.5
  132.2 5.7 %copy-done.5 = bf16[16,64,8192]{2,1,0:T(8,128)(2,1)} copy-done((bf16[16,64,8192]{2,1,0:T(8,128)(2,1)}, bf16[16,64,8192]{2,1,0:T(8,128)(2,1)S(1)}, u32[]{:S(2)}) %copy-start.5) | copy-done | bytes 16777240
  137.9 0.0 slice-start.1
  137.9 20.2 %convolution_convert_fusion.kv_ref = bf16[704,8192]{1,0:T(8,128)(2,1)} fusion(bf16[704,1024]{1,0:T(8,128)(2,1)S(1)} %bitcast.19, bf16[1024,8192]{1,0:T(8,128)(2,1)} %bitcast.17), kind=kOutput, calls=%fused_computation | convolution fusion | flops 11816927232 | bytes 29753344 | tf_op jit(solution)/shard_map/dot_general | solution.py:500
  158.2 0.0 slice-done
  158.2 0.0 slice-done.1
  158.2 0.0 copy-start
  158.2 2.6 copy-done
  160.8 28.6 %shard_map.78 = (bf16[704,4096]{1,0:T(8,128)(2,1)}, bf16[704,8192]{1,0:T(8,128)(2,1)}) custom-call(bf16[704,4096]{1,0:T(8,128)(2,1)S(1)} %bitcast.13, bf16[704,4096]{1,0:T(8,128)(2,1)S(1)} %copy-done, bf16[704,8192]{1,0:T(8,128)(2,1)} %convolution_convert_fusion.kv_ref), custom_call_target="tpu_custom_call" | custom-call | tf_op jit(solution)/shard_map/pallas_call | solution.py:472
  189.4 0.0 copy-start.2
  189.4 0.0 copy-start.4
  189.4 17.4 %fusion.12.partial_ref = f32[22,32,1024]{2,1,0:T(8,128)S(1)} fusion(bf16[22,32,8192]{2,1,0:T(8,128)(2,1)} %bitcast.21, bf16[1024,8192,1]{1,0,2:T(8,128)(2,1)} %bitcast.18), kind=kOutput, calls=%fused_computation.33 | convolution fusion | flops 11811160064 | bytes 31195136 | tf_op jit(solution)/shard_map/dot_general | solution.py:502
  206.8 0.0 copy-done.2
  206.8 0.0 copy-done.4
  206.8 87.4 %shard_map.79 = bf16[22,32,512]{2,1,0:T(8,128)(2,1)S(1)} custom-call(s32[32]{0:T(128)S(1)} %get-tuple-element.12.back_ref, s32[22]{0:T(128)S(1)} %dynamic_slice.3.take_ref, f32[22,32,1024]{2,1,0:T(8,128)S(1)} %fusion.12.partial_ref, bf16[22,32,512]{2,1,0:T(8,128)(2,1)S(1)} %copy-done.2, f32[22,32,1]{2,1,0:T(8,128)S(1)} %get-tuple-element.11.rms_ref, ...), custom_call_target="tpu_custom_call" | custom-call | tf_op jit(solution)/shard_map/pallas_call | solution.py:143
  294.3 0.9 copy.10
  (2 shorter events, 0.0 us)
Async XLA Ops:
  5.6 1.1 copy-start.1
  6.7 0.7 copy-start.3
  7.4 150.8 %slice-start = ((s8[5767168]{0:T(1024)(128)(4,1)}), s8[4194304]{0:T(1024)(128)(4,1)S(1)}, s32[]{:S(2)}) async-start(s8[5767168]{0:T(1024)(128)(4,1)} %bitcast.12), calls=%async_computation | async-start | bytes 8388608
  132.2 5.7 %copy-start.5 = (bf16[16,64,8192]{2,1,0:T(8,128)(2,1)}, bf16[16,64,8192]{2,1,0:T(8,128)(2,1)S(1)}, u32[]{:S(2)}) copy-start(bf16[16,64,8192]{2,1,0:T(8,128)(2,1)S(1)} %get-tuple-element.8) | copy-start | bytes 50331652
  137.9 20.2 %slice-start.1 = ((s8[5767168]{0:T(1024)(128)(4,1)}), s8[1572864]{0:T(1024)(128)(4,1)S(1)}, s32[]{:S(2)}) async-start(s8[5767168]{0:T(1024)(128)(4,1)} %bitcast.12), calls=%async_computation.1 | async-start | bytes 3145728
  158.2 2.6 copy-start
  189.4 17.5 %copy-start.2 = (bf16[22,32,512]{2,1,0:T(8,128)(2,1)S(1)}, bf16[22,32,512]{2,1,0:T(8,128)(2,1)}, u32[]{:S(2)}) copy-start(bf16[22,32,512]{2,1,0:T(8,128)(2,1)} %x_ref.3) | copy-start | bytes 2162692
  189.4 17.5 %copy-start.4 = (f32[512]{0:T(512)S(1)}, f32[512]{0:T(512)}, u32[]{:S(2)}) copy-start(f32[512]{0:T(512)} %param.8) | copy-start | bytes 6148

commit v2 on v1

--- a/solution.py
+++ b/solution.py
@@ -103,11 +103,12 @@
         parcel(d).wait_recv()
 
     gain = gain_ref[...]
+    mine[...] = jnp.zeros_like(mine)
 
     @pl.loop(0, per_dev)
     def _(i):
         scaled = gain * arrived[take_ref[i]].astype(jnp.float32)
-        mine[i] = fold(x_ref[i].astype(jnp.float32) * scaled)
+        put_column(mine, i, fold(x_ref[i].astype(jnp.float32) * scaled))
 
     inners = []
     for d in range(1, heads):
@@ -119,10 +120,10 @@
 
     @pl.loop(0, per_dev)
     def _(i):
-        total = mine[i]
+        total = mine[...]
         for d in range(1, heads):
-            total = total + others[d - 1, i]
-        inner = jnp.sum(total, axis=-1, keepdims=True) / (ew_part * heads)
+            total = total + others[d - 1]
+        inner = column(total, i) / (ew_part * heads)
         scaled = gain * arrived[take_ref[i]].astype(jnp.float32)
         rms = rms_ref[i]
         x = x_ref[i].astype(jnp.float32)
@@ -151,8 +152,8 @@
             pltpu.VMEM(x.shape, jnp.bfloat16),
             pltpu.VMEM((slots, nlen, ew_part), jnp.bfloat16),
             pltpu.VMEM((slots, nlen, ew_part), jnp.bfloat16),
-            pltpu.VMEM((per_dev, nlen, HEAD_DIM), jnp.float32),
-            pltpu.VMEM((heads - 1, per_dev, nlen, HEAD_DIM), jnp.float32),
+            pltpu.VMEM((nlen, HEAD_DIM), jnp.float32),
+            pltpu.VMEM((heads - 1, nlen, HEAD_DIM), jnp.float32),
             pltpu.SemaphoreType.DMA,
             pltpu.SemaphoreType.DMA((heads - 1,)),
             pltpu.SemaphoreType.DMA((heads - 1,)),
@@ -207,6 +208,16 @@
 
 ACROSS = 4
 CORES = 2
+
+
+def put_column(ref, i, values):
+    lane = lax.broadcasted_iota(jnp.int32, ref.shape, 1)
+    ref[...] = jnp.where(lane == i, jnp.sum(values, axis=-1, keepdims=True), ref[...])
+
+
+def column(total, i):
+    lane = lax.broadcasted_iota(jnp.int32, total.shape, 1)
+    return jnp.sum(jnp.where(lane == i, total, 0.0), axis=-1, keepdims=True)
 
 
 def gather_kernel(
@@ -296,10 +307,12 @@
     moves(a, b, 0, 0, True, start)
     own_copy.start()
 
+    mine[...] = jnp.zeros_like(mine)
+
     @pl.loop(0, per_dev)
     def _(i):
         x = x_ref[i].astype(jnp.float32)
-        mine[i] = fold(x * x)
+        put_column(mine, i, fold(x * x))
 
     squares = []
     for d in range(1, heads):
@@ -312,10 +325,10 @@
 
     @pl.loop(0, per_dev)
     def _(i):
-        total = mine[i]
+        total = mine[...]
         for d in range(1, heads):
-            total = total + others[d - 1, i]
-        mean = jnp.sum(total, axis=-1, keepdims=True) / (ew_part * heads)
+            total = total + others[d - 1]
+        mean = column(total, i) / (ew_part * heads)
         rms = lax.rsqrt(mean + 1e-05)
         rms_ref[i] = rms
         normed[i] = (x_ref[i].astype(jnp.float32) * rms * gain).astype(jnp.bfloat16)
@@ -390,8 +403,8 @@
         in_specs=[smem, smem, anywhere, vmem, vmem],
         out_specs=(anywhere, anywhere, vmem),
         scratch_shapes=[
-            pltpu.VMEM((per_dev, nlen, HEAD_DIM), jnp.float32),
-            pltpu.VMEM((heads - 1, per_dev, nlen, HEAD_DIM), jnp.float32),
+            pltpu.VMEM((nlen, HEAD_DIM), jnp.float32),
+            pltpu.VMEM((heads - 1, nlen, HEAD_DIM), jnp.float32),
             pltpu.VMEM(x.shape, jnp.bfloat16),
             pltpu.VMEM((slots, nlen, ew_part), jnp.bfloat16),
             pltpu.VMEM((slots, nlen, ew_part), jnp.bfloat16),

time: 295 us -> 290 us (0.983)
  Pallas kernels: 241 us -> 235 us
    pallas_call x1, Pallas kernels: 87.4 us -> 81.6 us  [tail(): pl.pallas_call(functools.partial(tail_kernel, n, heads), out_shape=jax.Sh...]
where the time goes in v2:
time: 290 us; the launch traced here: 289 us
  Pallas kernels  235 us (81%)
  matrix products  38 us (13%)
  local copies, waits for them, and re-layouts  12.9 us (4%)
    pallas_call x1, Pallas kernels, gather(): pl.pallas_call(functools.partial(gather_kernel, n, heads), out_shape=(jax...  125 us
    pallas_call x1, Pallas kernels, tail(): pl.pallas_call(functools.partial(tail_kernel, n, heads), out_shape=jax.Sh...  81.6 us
    pallas_call x1, Pallas kernels, attention(): pl.pallas_call(attention_kernel, grid=(rows // SPAN,), out_shape=(jax.Sha...  28.6 us
    dot_general x1, matrix products, shards(): jnp.dot(full_rows, weights, preferred_element_type=jnp.float32)  20.2 us
    dot_general x1, matrix products, shards(): lax.dot_general(grad_kv, weights, (((1,), (1,)), ((), ())), preferred_ele...  17.4 us
    unnamed x18, local copies, waits for them, and re-layouts  12.8 us

profile of v2, /device:TPU:13, one launch (start us, length us, event | category | flops | bytes accessed | tf_op | source)
XLA Modules:
  0.0 289.3 jit_solution(4627505074424382529)
XLA Ops:
  0.6 1.0 convert_reduce_fusion
  1.6 0.7 broadcast_compare_fusion
  2.3 0.3 convert_reduce_fusion.1
  2.6 0.7 multiply_add_fusion
  3.3 0.3 multiply_reduce_fusion
  3.6 0.1 dynamic_slice.3.take_ref
  3.7 0.1 select_reduce_fusion.send_ref
  3.8 1.8 copy.8
  5.6 0.0 copy-start.1
  5.6 1.1 copy-done.1
  6.7 0.0 copy-start.3
  6.7 0.7 copy-done.3
  7.4 0.0 slice-start
  7.4 124.8 %shard_map.77 = (bf16[16,64,8192]{2,1,0:T(8,128)(2,1)S(1)}, bf16[22,32,1024]{2,1,0:T(8,128)(2,1)S(1)}, f32[22,32,1]{2,1,0:T(8,128)S(1)}) custom-call(s32[32]{0:T(128)S(1)} %select_reduce_fusion.send_ref, s32[22]{0:T(128)S(1)} %get-tuple-element.13.take_ref, bf16[64,8192]{1,0:T(8,128)(2,1)S(1)} %bitcast.14, bf16[22,32,512]{2,1,0:T(8,128)(2,1)S(1)} %copy-done.1, ...), custom_call_target="tpu_custom_call" | custom-call | tf_op jit(solution)/shard_map/pallas_call | solution.py:396
  132.2 0.0 copy-start.5
  132.2 5.7 %copy-done.5 = bf16[16,64,8192]{2,1,0:T(8,128)(2,1)} copy-done((bf16[16,64,8192]{2,1,0:T(8,128)(2,1)}, bf16[16,64,8192]{2,1,0:T(8,128)(2,1)S(1)}, u32[]{:S(2)}) %copy-start.5) | copy-done | bytes 16777240
  137.9 0.0 slice-start.1
  137.9 20.2 %convolution_convert_fusion.kv_ref = bf16[704,8192]{1,0:T(8,128)(2,1)} fusion(bf16[704,1024]{1,0:T(8,128)(2,1)S(1)} %bitcast.19, bf16[1024,8192]{1,0:T(8,128)(2,1)} %bitcast.17), kind=kOutput, calls=%fused_computation | convolution fusion | flops 11816927232 | bytes 29753344 | tf_op jit(solution)/shard_map/dot_general | solution.py:513
  158.2 0.0 slice-done
  158.2 0.0 slice-done.1
  158.2 0.0 copy-start
  158.2 2.6 copy-done
  160.8 28.6 %shard_map.78 = (bf16[704,4096]{1,0:T(8,128)(2,1)}, bf16[704,8192]{1,0:T(8,128)(2,1)}) custom-call(bf16[704,4096]{1,0:T(8,128)(2,1)S(1)} %bitcast.13, bf16[704,4096]{1,0:T(8,128)(2,1)S(1)} %copy-done, bf16[704,8192]{1,0:T(8,128)(2,1)} %convolution_convert_fusion.kv_ref), custom_call_target="tpu_custom_call" | custom-call | tf_op jit(solution)/shard_map/pallas_call | solution.py:485
  189.4 0.0 copy-start.2
  189.4 0.0 copy-start.4
  189.4 17.4 %fusion.12.partial_ref = f32[22,32,1024]{2,1,0:T(8,128)S(1)} fusion(bf16[22,32,8192]{2,1,0:T(8,128)(2,1)} %bitcast.21, bf16[1024,8192,1]{1,0,2:T(8,128)(2,1)} %bitcast.18), kind=kOutput, calls=%fused_computation.33 | convolution fusion | flops 11811160064 | bytes 31195136 | tf_op jit(solution)/shard_map/dot_general | solution.py:515
  206.8 0.0 copy-done.2
  206.8 0.0 copy-done.4
  206.8 81.6 %shard_map.79 = bf16[22,32,512]{2,1,0:T(8,128)(2,1)S(1)} custom-call(s32[32]{0:T(128)S(1)} %get-tuple-element.12.back_ref, s32[22]{0:T(128)S(1)} %dynamic_slice.3.take_ref, f32[22,32,1024]{2,1,0:T(8,128)S(1)} %fusion.12.partial_ref, bf16[22,32,512]{2,1,0:T(8,128)(2,1)S(1)} %copy-done.2, f32[22,32,1]{2,1,0:T(8,128)S(1)} %get-tuple-element.11.rms_ref, ...), custom_call_target="tpu_custom_call" | custom-call | tf_op jit(solution)/shard_map/pallas_call | solution.py:144
  288.5 0.9 copy.10
  (2 shorter events, 0.0 us)
Async XLA Ops:
  5.6 1.1 copy-start.1
  6.7 0.7 copy-start.3
  7.4 150.8 %slice-start = ((s8[5767168]{0:T(1024)(128)(4,1)}), s8[4194304]{0:T(1024)(128)(4,1)S(1)}, s32[]{:S(2)}) async-start(s8[5767168]{0:T(1024)(128)(4,1)} %bitcast.12), calls=%async_computation | async-start | bytes 8388608
  132.2 5.7 %copy-start.5 = (bf16[16,64,8192]{2,1,0:T(8,128)(2,1)}, bf16[16,64,8192]{2,1,0:T(8,128)(2,1)S(1)}, u32[]{:S(2)}) copy-start(bf16[16,64,8192]{2,1,0:T(8,128)(2,1)S(1)} %get-tuple-element.8) | copy-start | bytes 50331652
  137.9 20.2 %slice-start.1 = ((s8[5767168]{0:T(1024)(128)(4,1)}), s8[1572864]{0:T(1024)(128)(4,1)S(1)}, s32[]{:S(2)}) async-start(s8[5767168]{0:T(1024)(128)(4,1)} %bitcast.12), calls=%async_computation.1 | async-start | bytes 3145728
  158.2 2.6 copy-start
  189.4 17.5 %copy-start.2 = (bf16[22,32,512]{2,1,0:T(8,128)(2,1)S(1)}, bf16[22,32,512]{2,1,0:T(8,128)(2,1)}, u32[]{:S(2)}) copy-start(bf16[22,32,512]{2,1,0:T(8,128)(2,1)} %x_ref.3) | copy-start | bytes 2162692
  189.4 17.5 %copy-start.4 = (f32[512]{0:T(512)S(1)}, f32[512]{0:T(512)}, u32[]{:S(2)}) copy-start(f32[512]{0:T(512)} %param.8) | copy-start | bytes 6148
